TPU v7x, 32 devices: a whole 2x2x4 slice. The times are simulated.
32 devices in a mesh: lat: 8 (over z, x), lev: 4 (over y, core).
Axes of the slice: x: 2, y: 2, z: 4, core: 2. Of those that a mesh axis runs over, the one named last changes fastest.
Arguments:
- particle_mass_fraction: float32 [20, 64, 8, 360], P(None, 'lat', 'lev'), may hold values from 0.1 to 2
- meridional_cfl_factor: float32 [64, 8, 360], P('lat', 'lev'), may hold values from -0.45 to 0.45
- thermal_state_kelvins: float32 [64, 8, 360], P('lat', 'lev'), may hold values from 200 to 300
- logarithmic_barometric_span: float32 [8], P('lev'), may hold values from 0.06 to 0.2
- gravitational_fall_kilometres: float32 [20], replicated, may hold values from 0.02 to 20
- zonal_cfl_factor: float32 [64, 8, 360], P('lat', None, 'lev'), may hold values from -0.45 to 0.45
- collision_rate_matrix: float32 [20, 20], replicated, may hold values from 0.02 to 0.2
Outputs:
- dust_out: float32 [20, 64, 8, 360], P(None, 'lat', None, 'lev')
- height: float32 [64, 8, 360], P('lat', 'lev')
All inputs are finite; a program needn't handle non-finite values.
Results may differ from a plain program's by a relative error of at most 0.000067.
Values sent between devices are 32-bit elements; how exact they have to be, the bound alone decides.
A program may use at most 128 MiB of HBM per device.

v0:
```python
import jax
import jax.numpy as jnp
from jax import lax
from jax.sharding import PartitionSpec as P

specific_air_factor = 0.0293
scale_height = 7.0


def extended_2(x, sides, width, wrap):
    for axis, dim in sides:
        peers, length = (lax.axis_size(axis), x.shape[dim])
        up = [(i, (i + 1) % peers) for i in range(peers if wrap else peers - 1)]
        down = [(j, i) for i, j in up]
        last = lax.slice_in_dim(x, length - width, length, axis=dim)
        leading = lax.slice_in_dim(x, 0, width, axis=dim)
        before = lax.ppermute(last, axis, up)
        after = lax.ppermute(leading, axis, down)
        x = jnp.concatenate([before, x, after], axis=dim)
    return x


def prefix(value, axis, join, neutral):
    count, mine = (lax.axis_size(axis), lax.axis_index(axis))
    pieces = lax.all_gather(value, axis)
    pieces = pieces[::-1]
    mine = count - 1 - mine
    subtotal = jnp.full_like(value, 0) + jnp.asarray(neutral, value.dtype)

    def step(position, subtotal):
        longer = join(subtotal, pieces[position])
        return jnp.where(position < mine, longer, subtotal)

    return lax.fori_loop(0, count - 1, step, subtotal)


def settle_sweep(mixing, settle_rate, inflow):

    def stepper(flux_in, inputs):
        level_mix, level_rate = inputs
        summed = level_mix + flux_in
        return (level_rate / (1.0 + level_rate) * summed, summed / (1.0 + level_rate))

    _, swept = lax.scan(
        stepper, inflow, (jnp.moveaxis(mixing, 2, 0), jnp.moveaxis(settle_rate, 2, 0))
    )
    return jnp.moveaxis(swept, 0, 2)


def add_terms(earlier, later):
    return earlier + later


def on_device(
    particle_mass_fraction,
    meridional_cfl_factor,
    thermal_state_kelvins,
    logarithmic_barometric_span,
    gravitational_fall_kilometres,
    zonal_cfl_factor,
    collision_rate_matrix,
):
    bin_count = particle_mass_fraction.shape[0]
    stacked = jnp.concatenate([particle_mass_fraction, meridional_cfl_factor[None]], 0)
    padded = extended_2(stacked, (("lat", 1),), 1, False)
    rows_below = padded[:bin_count, :-2]
    rows_above = padded[:bin_count, 2:]
    courant_above = padded[bin_count, 2:]
    south_flux = (
        jnp.maximum(meridional_cfl_factor, 0.0) * rows_below
        + jnp.minimum(meridional_cfl_factor, 0.0) * particle_mass_fraction
    )
    north_flux = (
        jnp.maximum(courant_above, 0.0) * particle_mass_fraction
        + jnp.minimum(courant_above, 0.0) * rows_above
    )
    advected = particle_mass_fraction + south_flux - north_flux
    vertical_span_height = (
        specific_air_factor * thermal_state_kelvins * logarithmic_barometric_span[None, :, None]
    )
    column_total = jnp.sum(vertical_span_height, axis=1)
    incoming = prefix(column_total, "lev", add_terms, jnp.zeros_like(column_total))
    height = (
        incoming[:, None, :]
        + jnp.cumsum(vertical_span_height[:, ::-1], axis=1)[:, ::-1]
        - 0.5 * vertical_span_height
    )
    density = jnp.exp(-height / scale_height)
    packed = jnp.concatenate([advected, vertical_span_height[None], density[None]], 0)
    columns = lax.all_to_all(packed, "lev", split_axis=3, concat_axis=2, tiled=True)
    col_thick = columns[bin_count]
    col_density = columns[bin_count + 1]
    settle_rate = gravitational_fall_kilometres[:, None, None, None] / col_thick[None]
    inflow = jnp.zeros((bin_count, columns.shape[1], columns.shape[3]), jnp.float32)
    settled = settle_sweep(columns[:bin_count], settle_rate, inflow)
    extended = extended_2(
        jnp.concatenate([settled, zonal_cfl_factor[None]], 0), (("lev", 3),), 1, True
    )
    west_mix = extended[:bin_count, :, :, :-2]
    east_mix = extended[:bin_count, :, :, 2:]
    courant_east = extended[bin_count, :, :, 2:]
    west_flux = (
        jnp.maximum(zonal_cfl_factor, 0.0) * west_mix + jnp.minimum(zonal_cfl_factor, 0.0) * settled
    )
    east_flux = jnp.maximum(courant_east, 0.0) * settled + jnp.minimum(courant_east, 0.0) * east_mix
    moved = settled + west_flux - east_flux
    merging = jnp.tril(collision_rate_matrix, -1) - jnp.triu(collision_rate_matrix, 1)
    coag_rate = jnp.einsum("bc,clkx->blkx", merging, moved, precision=lax.Precision.HIGHEST)
    return (moved + col_density * moved * coag_rate, height)


def solution(mesh):
    in_specs = (
        P(None, "lat", "lev", None),
        P("lat", "lev", None),
        P("lat", "lev", None),
        P("lev"),
        P(),
        P("lat", None, "lev"),
        P(),
    )
    out_specs = (P(None, "lat", None, "lev"), P("lat", "lev", None))
    return jax.shard_map(
        on_device, mesh=mesh, in_specs=in_specs, out_specs=out_specs, check_vma=False
    )
```

profile of v0, /device:TPU:0, one launch (start us, length us, event | category | flops | bytes accessed | tf_op | source)
XLA Modules:
  0.0 57.4 jit_solution(17528665692314259171)
XLA Ops:
  0.6 1.0 %pad_maximum_fusion.11 = (f32[21,1,2,360]{3,2,1,0:T(2,128)S(1)}, f32[21,1,2,360]{3,2,1,0:T(2,128)S(1)}) fusion(f32[1,8,2,360]{3,2,1,0:T(2,128)} %bitcast.67, f32[20,8,2,360]{3,2,1,0:T(2,128)} %param.11), kind=kLoop, calls=%fused_computation.41 | loop fusion | flops 30240 | bytes 604800 | tf_op jit(solution)/shard_map/slice | solution.py:15
  1.7 1.3 %collective-permute-start.1 = (f32[21,1,2,360]{3,2,1,0:T(2,128)S(1)}, f32[21,1,2,360]{3,2,1,0:T(2,128)S(1)}, u32[]{:S(2)}, u32[]{:S(2)}) collective-permute-start(f32[21,1,2,360]{3,2,1,0:T(2,128)S(1)} %get-tuple-element.233), channel_id=1, source_target_pairs={{4,0},{8,4},{12,8},{16,12},{20,16},{24,20},{28,24},{5,1},{9,5},{13... | collective-permute-start | bytes 181448 | tf_op jit(solution)/shard_map/ppermute | solution.py:18
  3.0 5.5 %collective-permute-start = (f32[21,1,2,360]{3,2,1,0:T(2,128)S(1)}, f32[21,1,2,360]{3,2,1,0:T(2,128)S(1)}, u32[]{:S(2)}, u32[]{:S(2)}) collective-permute-start(f32[21,1,2,360]{3,2,1,0:T(2,128)S(1)} %get-tuple-element.232), channel_id=1, source_target_pairs={{0,4},{4,8},{8,12},{12,16},{16,20},{20,24},{24,28},{1,5},{5,9},{9,... | collective-permute-start | bytes 181448 | tf_op jit(solution)/shard_map/ppermute | solution.py:17
  8.4 0.8 %broadcast_maximum_fusion.2 = (f32[8,2,360]{2,1,0:T(2,128)S(1)}, f32[8,2,360]{2,1,0:T(2,128)S(1)}) fusion(f32[8,2,360]{2,1,0:T(2,128)} %param.12), kind=kLoop, calls=%fused_computation.60 | loop fusion | flops 11520 | bytes 69120 | tf_op jit(solution)/shard_map/max | solution.py:70
  9.2 0.7 %broadcast_multiply_fusion = f32[2]{0:T(128)S(1)} fusion(f32[2]{0:T(128)} %param.14), kind=kLoop, calls=%fused_computation.64 | loop fusion | flops 2 | bytes 16 | tf_op jit(solution)/shard_map/mul | solution.py:79
  9.9 0.8 %fusion.29 = (f32[8,360]{1,0:T(8,128)S(1)}, f32[8,2,360]{2,0,1:T(8,128)S(1)}) fusion(f32[2]{0:T(128)S(1)} %broadcast_multiply_fusion, f32[8,2,360]{2,1,0:T(2,128)} %param.13), kind=kLoop, calls=%fused_computation.67 | loop fusion | flops 8640 | bytes 57608 | tf_op jit(solution)/shard_map/reduce_sum | solution.py:81
  10.8 5.3 %all-gather = f32[32,360]{1,0:T(8,128)S(1)} all-gather(f32[8,360]{1,0:T(8,128)S(1)} %get-tuple-element.224), channel_id=2, replica_groups=mesh['lat'=8,'lev'=4] {'lev'}, dimensions={0}, use_global_device_ids=true | all-gather | bytes 57600 | tf_op jit(solution)/shard_map/all_gather | solution.py:25
  16.2 0.6 %exponential_bitcast_fusion = (f32[1,8,2,360]{3,1,2,0:T(8,128)S(1)}, f32[8,2,360]{2,0,1:T(8,128)}) fusion(f32[8,2,360]{2,0,1:T(8,128)S(1)} %get-tuple-element.225, f32[8,2,360]{2,0,1:T(8,128)S(1)} %fusion.31, f32[8,360]{1,0:T(8,128)S(1)} %get-tuple-element.108), kind=kLoop, calls=%fused_computation.45 | loop fusion | flops 28800 | bytes 103680 | tf_op jit(solution)/shard_map/broadcast_in_dim | solution.py:89
  16.8 0.8 %maximum_bitcast_fusion = (f32[8,2,360]{2,1,0:T(2,128)S(1)}, f32[1,8,2,360]{3,2,1,0:T(2,128)S(1)}) fusion(f32[21,1,2,360]{3,2,1,0:T(2,128)S(1)} %collective-permute-done.1, f32[1,8,2,360]{3,2,1,0:T(2,128)} %bitcast.68, f32[20,8,2,360]{3,2,1,0:T(2,128)} %param.11), kind=kLoop, calls=%fused_computation.48 | loop fusion | flops 17280 | bytes 590400 | tf_op jit(solution)/shard_map/mul | solution.py:74
  17.7 1.7 %pad_maximum_fusion.8 = (f32[20,8,2,360]{3,2,1,0:T(2,128)S(1)}, f32[20,8,2,360]{3,2,1,0:T(2,128)S(1)}) fusion(f32[21,1,2,360]{3,2,1,0:T(2,128)S(1)} %collective-permute-done, f32[1,8,2,360]{3,2,1,0:T(2,128)} %bitcast.69, f32[20,8,2,360]{3,2,1,0:T(2,128)} %param.11, f32[21,1,2,360]{3,2,1,0:T(2,128)S(1)} %collective-permute-done.1), kind=kLoop, calls=%fused_computation.27 | loop fusion | flops 460800 | bytes 1526400 | tf_op jit(solution)/shard_map/concatenate | solution.py:19
  19.6 1.3 %copy.255 = f32[22,8,2,360]{0,1,2,3:T(8,128)S(1)} copy(f32[22,8,2,360]{3,1,2,0:T(8,128)S(1)} %pad_maximum_fusion.5) | data formatting | bytes 1013760 | tf_op jit(solution)/shard_map/concatenate | solution.py:89
  20.9 3.7 %reshape.18 = f32[4,1,31680]{2,1,0:T(1,128)} reshape(f32[360,2,8,22]{3,2,1,0:T(8,128)S(1)} %bitcast.60) | data formatting | bytes 1013760
  24.6 3.5 %all-to-all-start = ((f32[4,1,31680]{2,1,0:T(1,128)}), f32[4,1,31680]{2,1,0:T(1,128)S(1)}, u32[]{:S(2)}, u32[]{:S(2)}) async-start(f32[4,1,31680]{2,1,0:T(1,128)} %reshape.18), calls=%async_computation | async-start | bytes 1015808 | tf_op jit(solution)/shard_map/all_to_all | solution.py:90
  28.1 0.6 %broadcast_maximum_fusion.1 = (f32[8,8,90]{2,1,0:T(8,128)}, f32[8,8,90]{2,1,0:T(8,128)}) fusion(f32[8,8,90]{2,1,0:T(8,128)S(1)} %copy-done.2), kind=kLoop, calls=%fused_computation.52 | loop fusion | flops 11520 | bytes 69120 | tf_op jit(solution)/shard_map/max | solution.py:103
  28.7 8.1 %all-to-all-done = f32[4,1,31680]{2,1,0:T(1,128)S(1)} async-done(((f32[4,1,31680]{2,1,0:T(1,128)}), f32[4,1,31680]{2,1,0:T(1,128)S(1)}, u32[]{:S(2)}, u32[]{:S(2)}) %all-to-all-start) | async-done | bytes 506912 | tf_op jit(solution)/shard_map/all_to_all | solution.py:90
  36.8 0.6 %broadcast.65 = f32[]{:T(128)} broadcast(f32[]{:T(128)} %constant.131), dimensions={} | broadcast | bytes 8 | tf_op jit(solution)/shard_map/all_to_all | solution.py:90
  37.4 2.2 %reduce = f32[4,31680]{1,0:T(4,128)S(1)} reduce(f32[4,1,31680]{2,1,0:T(1,128)S(1)} %all-to-all-done, f32[]{:T(128)} %broadcast.65), dimensions={1}, to_apply=%all_to_all.11.reduce_sub_computation | reduce | bytes 1013764 | tf_op jit(solution)/shard_map/all_to_all | solution.py:90
  39.6 3.5 %reshape.19 = f32[360,2,8,22]{3,2,1,0:T(8,128)S(1)} reshape(f32[4,31680]{1,0:T(4,128)S(1)} %reduce) | data formatting | bytes 1013760
  43.1 2.2 %copy.270 = f32[22,8,2,4,90]{4,3,1,2,0:T(4,128)} copy(f32[22,8,2,4,90]{0,1,2,4,3:T(8,128)S(1)} %bitcast.59) | data formatting | bytes 1013760 | tf_op jit(solution)/shard_map/all_to_all | solution.py:90
  45.3 0.8 %fusion.30 = (f32[1,8,4,2,90]{4,2,1,3,0:T(4,128)S(1)}, f32[1,8,4,2,90]{4,2,1,3,0:T(4,128)S(1)}) fusion(f32[22,8,4,2,90]{4,2,1,3,0:T(4,128)} %bitcast.65), kind=kLoop, calls=%fused_computation.68 | loop fusion | bytes 92160 | tf_op jit(solution)/shard_map/slice | solution.py:92
  46.1 1.1 %slice.65 = f32[20,8,4,2,90]{4,2,1,3,0:T(4,128)S(1)} slice(f32[22,8,4,2,90]{4,2,1,3,0:T(4,128)} %bitcast.66), slice={[0:20], [0:8], [0:4], [0:2], [0:90]} | slice | bytes 921600 | tf_op jit(solution)/shard_map/slice | solution.py:95
  47.5 0.8 %while.28 = (s32[]{:T(128)}, f32[20,8,90]{2,1,0:T(8,128)S(1)}, f32[8,20,8,90]{3,2,1,0:T(8,128)S(1)}, f32[8,20,8,90]{3,2,1,0:T(8,128)S(1)}, f32[8,20,8,90]{3,2,1,0:T(8,128)S(1)}, /*index=5*/s32[]{:T(128)}, s32[]{:T(128)}) while((s32[]{:T(128)}, f32[20,8,90]{2,1,0:T(8,128)S(1)}, f32[8,20,8,90]{3,2,1,0:T(8,128)S(1)}, ...), condition=%wide.region_5.6_spmd.clone, body=%wide.region_4.5_spmd.clone.sunk | while | flops 129603 | bytes 558176 | solution.py:44
  48.5 0.4 slice_maximum_fusion
  48.9 0.5 copy.263
  49.4 0.6 %copy.268 = f32[8,2,360]{2,1,0:T(2,128)} copy(f32[8,2,360]{2,0,1:T(8,128)S(1)} %copy-done.4) | data formatting | bytes 46080
  50.0 0.5 copy.261
  50.5 0.7 %collective-permute-start.2 = (f32[21,8,8,1]{0,2,3,1:T(8,128)S(1)}, f32[21,8,8,1]{0,2,3,1:T(8,128)S(1)}, u32[]{:S(2)}, u32[]{:S(2)}) collective-permute-start(f32[21,8,8,1]{0,2,3,1:T(8,128)S(1)} %copy.261), channel_id=1, source_target_pairs={{0,1},{1,2},{2,3},{3,0},{4,5},{5,6},{6,7},{7,4},{8,9},{9,10},{10,1... | collective-permute-start | bytes 16136 | tf_op jit(solution)/shard_map/ppermute | solution.py:17
  51.2 0.5 copy.264
  52.0 2.0 %collective-permute-done.2 = f32[21,8,8,1]{0,2,3,1:T(8,128)S(1)} collective-permute-done((f32[21,8,8,1]{0,2,3,1:T(8,128)S(1)}, f32[21,8,8,1]{0,2,3,1:T(8,128)S(1)}, u32[]{:S(2)}, u32[]{:S(2)}) %collective-permute-start.2) | collective-permute-done | bytes 5408 | tf_op jit(solution)/shard_map/ppermute | solution.py:17
  54.1 0.5 copy.262
  54.6 1.9 %fusion.3 = f32[20,8,8,90]{3,0,2,1:T(8,128)S(1)} fusion(f32[21,8,8,1]{3,0,2,1:T(8,128)S(1)} %copy.264, f32[1,8,8,90]{3,0,2,1:T(1,128)S(1)} %bitcast.73, f32[20,8,8,90]{3,0,2,1:T(8,128)S(1)} %bitcast.63, f32[21,8,8,1]{3,0,2,1:T(8,128)S(1)} %copy.262, f32[8,8,90]{2,1,0:T(8,128)S(1)} %copy.266, f32[8,8,90]{2,1,0:T(8,128)S(1)} %bitcast.78, ...), kind=kOutput, calls=%fused_computation.8 | convolution fusion | flops 30760400 | bytes 1072272 | tf_op jit(solution)/shard_map/bc,clkx->blkx/dot_general | solution.py:108
  56.5 1.0 %copy.267 = f32[20,8,8,90]{3,2,1,0:T(8,128)} copy(f32[20,8,8,90]{3,0,2,1:T(8,128)S(1)} %fusion.3) | data formatting | bytes 921600
  (64 shorter events, 1.7 us)
Async XLA Ops:
  0.6 18.8 %copy-start = (f32[20,8,2,360]{3,2,1,0:T(2,128)S(1)}, f32[20,8,2,360]{3,2,1,0:T(2,128)}, u32[]{:S(2)}) copy-start(f32[20,8,2,360]{3,2,1,0:T(2,128)} %param.11) | copy-start | bytes 1382404
  1.7 15.2 %collective-permute-start.1 = (f32[21,1,2,360]{3,2,1,0:T(2,128)S(1)}, f32[21,1,2,360]{3,2,1,0:T(2,128)S(1)}, u32[]{:S(2)}, u32[]{:S(2)}) collective-permute-start(f32[21,1,2,360]{3,2,1,0:T(2,128)S(1)} %get-tuple-element.233), channel_id=1, source_target_pairs={{4,0},{8,4},{12,8},{16,12},{20,16},{24,20},{28,24},{5,1},{9,5},{13... | collective-permute-start | bytes 181448 | tf_op jit(solution)/shard_map/ppermute | solution.py:18
  3.0 14.7 %collective-permute-start = (f32[21,1,2,360]{3,2,1,0:T(2,128)S(1)}, f32[21,1,2,360]{3,2,1,0:T(2,128)S(1)}, u32[]{:S(2)}, u32[]{:S(2)}) collective-permute-start(f32[21,1,2,360]{3,2,1,0:T(2,128)S(1)} %get-tuple-element.232), channel_id=1, source_target_pairs={{0,4},{4,8},{8,12},{12,16},{16,20},{20,24},{24,28},{1,5},{5,9},{9,... | collective-permute-start | bytes 181448 | tf_op jit(solution)/shard_map/ppermute | solution.py:17
  20.9 7.2 %copy-start.2 = (f32[8,8,90]{2,1,0:T(8,128)S(1)}, f32[8,8,90]{2,1,0:T(8,128)}, u32[]{:S(2)}) copy-start(f32[8,8,90]{2,1,0:T(8,128)} %param.16) | copy-start | bytes 69124
  24.6 12.3 %all-to-all-start = ((f32[4,1,31680]{2,1,0:T(1,128)}), f32[4,1,31680]{2,1,0:T(1,128)S(1)}, u32[]{:S(2)}, u32[]{:S(2)}) async-start(f32[4,1,31680]{2,1,0:T(1,128)} %reshape.18), calls=%async_computation | async-start | bytes 1015808 | tf_op jit(solution)/shard_map/all_to_all | solution.py:90
  43.1 4.3 %copy-start.7 = (f32[20]{0:T(128)S(1)}, f32[20]{0:T(128)}, u32[]{:S(2)}) copy-start(f32[20]{0:T(128)} %param.15) | copy-start | bytes 244
  45.3 2.2 %copy-start.1 = (f32[8,20,8,90]{3,2,1,0:T(8,128)S(1)}, f32[8,20,8,90]{3,2,1,0:T(8,128)}, u32[]{:S(2)}) copy-start(f32[8,20,8,90]{3,2,1,0:T(8,128)} %custom-call.2) | copy-start | bytes 1382404
  47.3 1.1 %copy-start.3 = (f32[8,8,90]{2,1,0:T(8,128)S(1)}, f32[8,8,90]{2,1,0:T(8,128)}, u32[]{:S(2)}) copy-start(f32[8,8,90]{2,1,0:T(8,128)} %param.16) | copy-start | bytes 69124
  48.3 1.1 %copy-start.4 = (f32[8,2,360]{2,0,1:T(8,128)S(1)}, f32[8,2,360]{2,0,1:T(8,128)}, u32[]{:S(2)}) copy-start(f32[8,2,360]{2,0,1:T(8,128)} %get-tuple-element.223) | copy-start | bytes 69124
  48.8 5.7 %copy-start.5 = (f32[8,8,90]{2,1,0:T(8,128)S(1)}, f32[8,8,90]{2,1,0:T(8,128)}, u32[]{:S(2)}) copy-start(f32[8,8,90]{2,1,0:T(8,128)} %get-tuple-element.234) | copy-start | bytes 69124
  48.8 5.7 %copy-start.6 = (f32[8,8,90]{2,1,0:T(8,128)S(1)}, f32[8,8,90]{2,1,0:T(8,128)}, u32[]{:S(2)}) copy-start(f32[8,8,90]{2,1,0:T(8,128)} %get-tuple-element.235) | copy-start | bytes 69124
  48.9 5.7 %copy-start.8 = (f32[20,20]{1,0:T(8,128)S(1)}, f32[20,20]{1,0:T(8,128)}, u32[]{:S(2)}) copy-start(f32[20,20]{1,0:T(8,128)} %param.17) | copy-start | bytes 4804
  49.3 1.9 %collective-permute-start.3 = (f32[21,8,8,1]{0,2,3,1:T(8,128)S(1)}, f32[21,8,8,1]{0,2,3,1:T(8,128)S(1)}, u32[]{:S(2)}, u32[]{:S(2)}) collective-permute-start(f32[21,8,8,1]{0,2,3,1:T(8,128)S(1)} %copy.263), channel_id=1, source_target_pairs={{1,0},{2,1},{3,2},{0,3},{5,4},{6,5},{7,6},{4,7},{9,8},{10,9},{11,1... | collective-permute-start | bytes 16136 | tf_op jit(solution)/shard_map/ppermute | solution.py:18
  50.5 3.5 %collective-permute-start.2 = (f32[21,8,8,1]{0,2,3,1:T(8,128)S(1)}, f32[21,8,8,1]{0,2,3,1:T(8,128)S(1)}, u32[]{:S(2)}, u32[]{:S(2)}) collective-permute-start(f32[21,8,8,1]{0,2,3,1:T(8,128)S(1)} %copy.261), channel_id=1, source_target_pairs={{0,1},{1,2},{2,3},{3,0},{4,5},{5,6},{6,7},{7,4},{8,9},{9,10},{10,1... | collective-permute-start | bytes 16136 | tf_op jit(solution)/shard_map/ppermute | solution.py:17
where the time goes:
time: 57.9 us; the launch traced here: 57.4 us
  local copies, waits for them, and re-layouts  17 us (29%)
  starting transfers between devices  11 us (19%)
  other arithmetic  10.8 us (19%)
  waiting for transfers between devices  10.1 us (17%)
  blocking collectives  5.29 us (9%)
  matrix products  1.89 us (3%)
  between operations  1.01 us (2%)
    unnamed x22, local copies, waits for them, and re-layouts  8.74 us
    all_to_all x1, waiting for transfers between devices, on_device(): lax.all_to_all(packed, 'lev', split_axis=3, concat_axis=2, tiled=True)  8.13 us
    ppermute x2, starting transfers between devices, extended_2(): before = lax.ppermute(last, axis, up)  6.16 us
    all_gather x1, blocking collectives, prefix(): pieces = lax.all_gather(value, axis)  5.29 us
    all_to_all x1, starting transfers between devices, on_device(): lax.all_to_all(packed, 'lev', split_axis=3, concat_axis=2, tiled=True)  3.47 us
    all_to_all x2, local copies, waits for them, and re-layouts, on_device(): lax.all_to_all(packed, 'lev', split_axis=3, concat_axis=2, tiled=True)  2.8 us
    all_to_all x1, other arithmetic, on_device(): lax.all_to_all(packed, 'lev', split_axis=3, concat_axis=2, tiled=True)  2.16 us
    ppermute x2, waiting for transfers between devices, extended_2(): before = lax.ppermute(last, axis, up)  2.01 us
  transfers between devices with their start and end apart: 5, of which 2 were waited for; matrix products, arithmetic and copies ran while one was open for 11% of the time, Pallas kernels for 0%

commit v1 on v0

--- a/solution.py
+++ b/solution.py
@@ -5,6 +5,22 @@
 
 specific_air_factor = 0.0293
 scale_height = 7.0
+
+
+def exchange_in_pairs(x, axis, split, join):
+    ways, here = (lax.axis_size(axis), lax.axis_index(axis))
+    width = x.shape[split] // ways
+    shape = list(x.shape)
+    shape[split] = width
+    height = shape[join]
+    shape[join] = height * ways
+    full = jnp.zeros(shape, x.dtype)
+    for mask in range(ways):
+        part = lax.dynamic_slice_in_dim(x, (here ^ mask) * width, width, axis=split)
+        if mask:
+            part = lax.ppermute(part, axis, [(d, d ^ mask) for d in range(ways)])
+        full = lax.dynamic_update_slice_in_dim(full, part, (here ^ mask) * height, axis=join)
+    return full
 
 
 def extended_2(x, sides, width, wrap):
@@ -87,7 +103,7 @@
     )
     density = jnp.exp(-height / scale_height)
     packed = jnp.concatenate([advected, vertical_span_height[None], density[None]], 0)
-    columns = lax.all_to_all(packed, "lev", split_axis=3, concat_axis=2, tiled=True)
+    columns = exchange_in_pairs(packed, "lev", 3, 2)
     col_thick = columns[bin_count]
     col_density = columns[bin_count + 1]
     settle_rate = gravitational_fall_kilometres[:, None, None, None] / col_thick[None]

time: 57.9 us -> 39.2 us (0.68)
  local copies, waits for them, and re-layouts: 17 us -> 6.25 us
  other arithmetic: 10.8 us -> 2.66 us
    all_to_all x1 -> x0, waiting for transfers between devices: 8.13 us -> none  [on_device(): lax.all_to_all(packed, 'lev', split_axis=3, concat_axis=2, tiled=True)]
    ppermute x0 -> x3, waiting for transfers between devices: none -> 8.06 us  [exchange_in_pairs(): part = lax.ppermute(part, axis, [(d, d ^ mask) for d in range(ways)])]
    unnamed x22 -> x15, local copies, waits for them, and re-layouts: 8.74 us -> 3.35 us
    all_to_all x1 -> x0, starting transfers between devices: 3.47 us -> none  [on_device(): lax.all_to_all(packed, 'lev', split_axis=3, concat_axis=2, tiled=True)]
    all_to_all x2 -> x0, local copies, waits for them, and re-layouts: 2.8 us -> none  [on_device(): lax.all_to_all(packed, 'lev', split_axis=3, concat_axis=2, tiled=True)]
    ppermute x0 -> x3, starting transfers between devices: none -> 2.45 us  [exchange_in_pairs(): part = lax.ppermute(part, axis, [(d, d ^ mask) for d in range(ways)])]
    all_to_all x1 -> x0, other arithmetic: 2.16 us -> none  [on_device(): lax.all_to_all(packed, 'lev', split_axis=3, concat_axis=2, tiled=True)]
    slice x4 -> x0, local copies, waits for them, and re-layouts: 1.99 us -> none  [the longest x1 1.14 us: on_device(): settled = settle_sweep(columns[:bin_count], settle_rate, inflow)]
  transfers between devices with their start and end apart: 5 -> 7, of which waited for: 2 -> 4; matrix products, arithmetic and copies ran while one was open for 11% -> 7% of each run, Pallas kernels for 0% -> 0%
where the time goes in v1:
time: 39.2 us; the launch traced here: 38.8 us
  starting transfers between devices  10.9 us (28%)
  waiting for transfers between devices  10.5 us (27%)
  local copies, waits for them, and re-layouts  6.25 us (16%)
  blocking collectives  5.29 us (13%)
  other arithmetic  2.66 us (7%)
  matrix products  1.82 us (5%)
  between operations  1.05 us (3%)
    ppermute x3, waiting for transfers between devices, exchange_in_pairs(): part = lax.ppermute(part, axis, [(d, d ^ mask) for d in range(ways)])  8.06 us
    ppermute x2, starting transfers between devices, extended_2(): before = lax.ppermute(last, axis, up)  5.51 us
    all_gather x1, blocking collectives, prefix(): pieces = lax.all_gather(value, axis)  5.29 us
    unnamed x15, local copies, waits for them, and re-layouts  3.35 us
    ppermute x2, starting transfers between devices, extended_2(): after = lax.ppermute(leading, axis, down)  2.97 us
    ppermute x3, starting transfers between devices, exchange_in_pairs(): part = lax.ppermute(part, axis, [(d, d ^ mask) for d in range(ways)])  2.45 us
    dot_general x1, matrix products, on_device(): jnp.einsum('bc,clkx->blkx', merging, moved, precision=lax.Precision.HIGHEST)  1.82 us
    ppermute x2, waiting for transfers between devices, extended_2(): before = lax.ppermute(last, axis, up)  1.42 us
  transfers between devices with their start and end apart: 7, of which 4 were waited for; matrix products, arithmetic and copies ran while one was open for 7% of the time, Pallas kernels for 0%

profile of v1, /device:TPU:0, one launch (start us, length us, event | category | flops | bytes accessed | tf_op | source)
XLA Modules:
  0.0 38.8 jit_solution(731074193727605036)
XLA Ops:
  0.6 1.1 %copy.26 = f32[20,8,2,360]{3,1,0,2:T(8,128)S(1)} copy(f32[20,8,2,360]{3,2,1,0:T(2,128)} %param.11) | data formatting | bytes 921600 | tf_op args[0]
  1.7 0.1 pad_maximum_fusion.11
  1.8 1.3 %collective-permute-start.1 = (f32[21,1,2,360]{3,1,0,2:T(1,128)S(1)}, f32[21,1,2,360]{3,1,0,2:T(1,128)S(1)}, u32[]{:S(2)}, u32[]{:S(2)}) collective-permute-start(f32[21,1,2,360]{3,1,0,2:T(1,128)S(1)} %get-tuple-element.182), channel_id=1, source_target_pairs={{4,0},{8,4},{12,8},{16,12},{20,16},{24,20},{28,24},{5,1},{9,5},{13... | collective-permute-start | bytes 181448 | tf_op jit(solution)/shard_map/ppermute | solution.py:34
  3.1 5.5 %collective-permute-start = (f32[21,1,2,360]{3,1,0,2:T(1,128)S(1)}, f32[21,1,2,360]{3,1,0,2:T(1,128)S(1)}, u32[]{:S(2)}, u32[]{:S(2)}) collective-permute-start(f32[21,1,2,360]{3,1,0,2:T(1,128)S(1)} %get-tuple-element.181), channel_id=1, source_target_pairs={{0,4},{4,8},{8,12},{12,16},{16,20},{20,24},{24,28},{1,5},{5,9},{9,... | collective-permute-start | bytes 181448 | tf_op jit(solution)/shard_map/ppermute | solution.py:33
  8.6 0.6 %copy-done.5 = f32[2]{0:T(128)S(1)} copy-done((f32[2]{0:T(128)S(1)}, f32[2]{0:T(128)}, u32[]{:S(2)}) %copy-start.5) | copy-done | bytes 32
  9.3 0.1 fusion.31
  9.4 5.3 %all-gather = f32[32,360]{1,0:T(8,128)S(1)} all-gather(f32[8,360]{1,0:T(8,128)S(1)} %get-tuple-element.171), channel_id=2, replica_groups=mesh['lat'=8,'lev'=4] {'lev'}, dimensions={0}, use_global_device_ids=true | all-gather | bytes 57600 | tf_op jit(solution)/shard_map/all_gather | solution.py:41
  14.7 0.1 while.27
  14.8 0.2 rev.10
  15.0 0.2 rev.11
  15.2 0.6 %exponential_bitcast_fusion = (f32[1,8,2,360]{3,2,1,0:T(2,128)S(1)}, f32[8,2,360]{2,1,0:T(2,128)}) fusion(f32[8,2,360]{2,1,0:T(2,128)S(1)} %get-tuple-element.172, f32[8,2,360]{2,1,0:T(2,128)S(1)} %rev.11, f32[8,360]{1,0:T(8,128)S(1)} %get-tuple-element.108), kind=kLoop, calls=%fused_computation.49 | loop fusion | flops 28800 | bytes 103680 | tf_op jit(solution)/shard_map/broadcast_in_dim | solution.py:105
  16.0 0.3 fusion.15
  16.4 0.3 constant_dynamic-slice_fusion
  16.7 0.4 %collective-permute-start.2 = (f32[22,8,2,90]{3,1,0,2:T(8,128)S(1)}, f32[22,8,2,90]{3,1,0,2:T(8,128)S(1)}, u32[]{:S(2)}, u32[]{:S(2)}) collective-permute-start(f32[22,8,2,90]{3,1,0,2:T(8,128)S(1)} %get-tuple-element.179), channel_id=1, source_target_pairs={{0,1},{1,0},{2,3},{3,2},{4,5},{5,4},{6,7},{7,6},{8,9},{9,8},{10,11... | collective-permute-start | bytes 380168 | tf_op jit(solution)/shard_map/ppermute | solution.py:21
  17.1 2.0 %collective-permute-start.3 = (f32[22,8,2,90]{3,1,0,2:T(8,128)S(1)}, f32[22,8,2,90]{3,1,0,2:T(8,128)S(1)}, u32[]{:S(2)}, u32[]{:S(2)}) collective-permute-start(f32[22,8,2,90]{3,1,0,2:T(8,128)S(1)} %get-tuple-element.178), channel_id=1, source_target_pairs={{0,2},{1,3},{2,0},{3,1},{4,6},{5,7},{6,4},{7,5},{8,10},{9,11},{10,... | collective-permute-start | bytes 380168 | tf_op jit(solution)/shard_map/ppermute | solution.py:21
  19.3 5.2 %collective-permute-done.3 = f32[22,8,2,90]{3,1,0,2:T(8,128)S(1)} collective-permute-done((f32[22,8,2,90]{3,1,0,2:T(8,128)S(1)}, f32[22,8,2,90]{3,1,0,2:T(8,128)S(1)}, u32[]{:S(2)}, u32[]{:S(2)}) %collective-permute-start.3) | collective-permute-done | bytes 126752 | tf_op jit(solution)/shard_map/ppermute | solution.py:21
  24.5 2.9 %collective-permute-done.4 = f32[22,8,2,90]{3,1,0,2:T(8,128)S(1)} collective-permute-done((f32[22,8,2,90]{3,1,0,2:T(8,128)S(1)}, f32[22,8,2,90]{3,1,0,2:T(8,128)S(1)}, u32[]{:S(2)}, u32[]{:S(2)}) %collective-permute-start.4) | collective-permute-done | bytes 126752 | tf_op jit(solution)/shard_map/ppermute | solution.py:21
  27.5 0.6 %copy-done.3 = f32[20]{0:T(128)S(1)} copy-done((f32[20]{0:T(128)S(1)}, f32[20]{0:T(128)}, u32[]{:S(2)}) %copy-start.3) | copy-done | bytes 104
  28.1 0.1 broadcast_divide_fusion
  28.2 0.8 %while.28 = (s32[]{:T(128)}, f32[20,8,90]{2,1,0:T(8,128)S(1)}, f32[8,20,8,90]{3,2,1,0:T(8,128)S(1)}, f32[8,20,8,90]{3,2,1,0:T(8,128)S(1)}, f32[8,20,8,90]{3,2,1,0:T(8,128)S(1)}, /*index=5*/s32[]{:T(128)}, s32[]{:T(128)}) while((s32[]{:T(128)}, f32[20,8,90]{2,1,0:T(8,128)S(1)}, f32[8,20,8,90]{3,2,1,0:T(8,128)S(1)}, ...), condition=%wide.region_5.6_spmd.clone, body=%wide.region_4.5_spmd.clone.sunk | while | flops 129603 | bytes 558176 | solution.py:60
  29.0 0.1 copy.40
  29.2 0.4 slice_maximum_fusion
  29.5 0.5 %copy.33 = f32[21,8,8,1]{0,2,3,1:T(8,128)S(1)} copy(f32[21,8,8,1]{3,0,2,1:T(8,128)S(1)} %get-tuple-element.174) | data formatting | bytes 10752 | tf_op jit(solution)/shard_map/slice | solution.py:32
  30.0 1.7 %collective-permute-start.6 = (f32[21,8,8,1]{0,2,3,1:T(8,128)S(1)}, f32[21,8,8,1]{0,2,3,1:T(8,128)S(1)}, u32[]{:S(2)}, u32[]{:S(2)}) collective-permute-start(f32[21,8,8,1]{0,2,3,1:T(8,128)S(1)} %copy.33), channel_id=1, source_target_pairs={{1,0},{2,1},{3,2},{0,3},{5,4},{6,5},{7,6},{4,7},{9,8},{10,9},{11,1... | collective-permute-start | bytes 16136 | tf_op jit(solution)/shard_map/ppermute | solution.py:34
  31.7 0.5 %copy.31 = f32[21,8,8,1]{0,2,3,1:T(8,128)S(1)} copy(f32[21,8,8,1]{3,0,2,1:T(8,128)S(1)} %get-tuple-element.173) | data formatting | bytes 10752 | tf_op jit(solution)/shard_map/slice | solution.py:31
  32.2 1.1 %collective-permute-done.6 = f32[21,8,8,1]{0,2,3,1:T(8,128)S(1)} collective-permute-done((f32[21,8,8,1]{0,2,3,1:T(8,128)S(1)}, f32[21,8,8,1]{0,2,3,1:T(8,128)S(1)}, u32[]{:S(2)}, u32[]{:S(2)}) %collective-permute-start.6) | collective-permute-done | bytes 5408 | tf_op jit(solution)/shard_map/ppermute | solution.py:34
  33.3 0.5 %copy.34 = f32[21,8,8,1]{3,0,2,1:T(8,128)S(1)} copy(f32[21,8,8,1]{0,2,3,1:T(8,128)S(1)} %collective-permute-done.6) | data formatting | bytes 10752 | tf_op jit(solution)/shard_map/ppermute | solution.py:34
  33.8 0.3 broadcast_maximum_fusion
  34.1 1.4 %collective-permute-done.5 = f32[21,8,8,1]{0,2,3,1:T(8,128)S(1)} collective-permute-done((f32[21,8,8,1]{0,2,3,1:T(8,128)S(1)}, f32[21,8,8,1]{0,2,3,1:T(8,128)S(1)}, u32[]{:S(2)}, u32[]{:S(2)}) %collective-permute-start.5) | collective-permute-done | bytes 5408 | tf_op jit(solution)/shard_map/ppermute | solution.py:33
  35.6 0.5 %copy.32 = f32[21,8,8,1]{3,0,2,1:T(8,128)S(1)} copy(f32[21,8,8,1]{0,2,3,1:T(8,128)S(1)} %collective-permute-done.5) | data formatting | bytes 10752 | tf_op jit(solution)/shard_map/ppermute | solution.py:33
  36.1 1.8 %fusion.3 = f32[20,8,8,90]{3,0,2,1:T(8,128)S(1)} fusion(f32[21,8,8,1]{3,0,2,1:T(8,128)S(1)} %copy.34, f32[1,8,8,90]{3,0,2,1:T(1,128)S(1)} %bitcast.66, f32[20,8,8,90]{3,0,2,1:T(8,128)S(1)} %bitcast.59, f32[21,8,8,1]{3,0,2,1:T(8,128)S(1)} %copy.32, f32[8,8,90]{2,1,0:T(8,128)S(1)} %copy.35, f32[8,8,90]{2,1,0:T(8,128)S(1)} %bitcast.69, ...), kind=kOutput, calls=%fused_computation.8 | convolution fusion | flops 30760400 | bytes 1072272 | tf_op jit(solution)/shard_map/bc,clkx->blkx/dot_general | solution.py:124
  37.9 1.0 %copy.36 = f32[20,8,8,90]{3,2,1,0:T(8,128)} copy(f32[20,8,8,90]{3,0,2,1:T(8,128)S(1)} %fusion.3) | data formatting | bytes 921600
  (59 shorter events, 1.1 us)
Async XLA Ops:
  0.6 1.1 %copy-start.1 = (f32[8,2,360]{2,1,0:T(2,128)S(1)}, f32[8,2,360]{2,1,0:T(2,128)}, u32[]{:S(2)}) copy-start(f32[8,2,360]{2,1,0:T(2,128)} %param.12) | copy-start | bytes 69124
  1.7 7.6 %copy-start.2 = (f32[8,2,360]{2,1,0:T(2,128)S(1)}, f32[8,2,360]{2,1,0:T(2,128)}, u32[]{:S(2)}) copy-start(f32[8,2,360]{2,1,0:T(2,128)} %param.13) | copy-start | bytes 69124
  1.8 14.1 %collective-permute-start.1 = (f32[21,1,2,360]{3,1,0,2:T(1,128)S(1)}, f32[21,1,2,360]{3,1,0,2:T(1,128)S(1)}, u32[]{:S(2)}, u32[]{:S(2)}) collective-permute-start(f32[21,1,2,360]{3,1,0,2:T(1,128)S(1)} %get-tuple-element.182), channel_id=1, source_target_pairs={{4,0},{8,4},{12,8},{16,12},{20,16},{24,20},{28,24},{5,1},{9,5},{13... | collective-permute-start | bytes 181448 | tf_op jit(solution)/shard_map/ppermute | solution.py:34
  3.1 12.9 %collective-permute-start = (f32[21,1,2,360]{3,1,0,2:T(1,128)S(1)}, f32[21,1,2,360]{3,1,0,2:T(1,128)S(1)}, u32[]{:S(2)}, u32[]{:S(2)}) collective-permute-start(f32[21,1,2,360]{3,1,0,2:T(1,128)S(1)} %get-tuple-element.181), channel_id=1, source_target_pairs={{0,4},{4,8},{8,12},{12,16},{16,20},{20,24},{24,28},{1,5},{5,9},{9,... | collective-permute-start | bytes 181448 | tf_op jit(solution)/shard_map/ppermute | solution.py:33
  8.6 0.7 %copy-start.5 = (f32[2]{0:T(128)S(1)}, f32[2]{0:T(128)}, u32[]{:S(2)}) copy-start(f32[2]{0:T(128)} %param.14) | copy-start | bytes 28
  16.4 2.7 %copy-start = (f32[8,8,90]{2,1,0:T(8,128)S(1)}, f32[8,8,90]{2,1,0:T(8,128)}, u32[]{:S(2)}) copy-start(f32[8,8,90]{2,1,0:T(8,128)} %param.16) | copy-start | bytes 69124
  16.7 2.5 %collective-permute-start.2 = (f32[22,8,2,90]{3,1,0,2:T(8,128)S(1)}, f32[22,8,2,90]{3,1,0,2:T(8,128)S(1)}, u32[]{:S(2)}, u32[]{:S(2)}) collective-permute-start(f32[22,8,2,90]{3,1,0,2:T(8,128)S(1)} %get-tuple-element.179), channel_id=1, source_target_pairs={{0,1},{1,0},{2,3},{3,2},{4,5},{5,4},{6,7},{7,6},{8,9},{9,8},{10,11... | collective-permute-start | bytes 380168 | tf_op jit(solution)/shard_map/ppermute | solution.py:21
  17.1 7.4 %collective-permute-start.3 = (f32[22,8,2,90]{3,1,0,2:T(8,128)S(1)}, f32[22,8,2,90]{3,1,0,2:T(8,128)S(1)}, u32[]{:S(2)}, u32[]{:S(2)}) collective-permute-start(f32[22,8,2,90]{3,1,0,2:T(8,128)S(1)} %get-tuple-element.178), channel_id=1, source_target_pairs={{0,2},{1,3},{2,0},{3,1},{4,6},{5,7},{6,4},{7,5},{8,10},{9,11},{10,... | collective-permute-start | bytes 380168 | tf_op jit(solution)/shard_map/ppermute | solution.py:21
  19.2 8.2 %collective-permute-start.4 = (f32[22,8,2,90]{3,1,0,2:T(8,128)S(1)}, f32[22,8,2,90]{3,1,0,2:T(8,128)S(1)}, u32[]{:S(2)}, u32[]{:S(2)}) collective-permute-start(f32[22,8,2,90]{3,1,0,2:T(8,128)S(1)} %get-tuple-element.177), channel_id=1, source_target_pairs={{0,3},{1,2},{2,1},{3,0},{4,7},{5,6},{6,5},{7,4},{8,11},{9,10},{10,... | collective-permute-start | bytes 380168 | tf_op jit(solution)/shard_map/ppermute | solution.py:21
  27.5 0.7 %copy-start.3 = (f32[20]{0:T(128)S(1)}, f32[20]{0:T(128)}, u32[]{:S(2)}) copy-start(f32[20]{0:T(128)} %param.15) | copy-start | bytes 244
  30.0 3.3 %collective-permute-start.6 = (f32[21,8,8,1]{0,2,3,1:T(8,128)S(1)}, f32[21,8,8,1]{0,2,3,1:T(8,128)S(1)}, u32[]{:S(2)}, u32[]{:S(2)}) collective-permute-start(f32[21,8,8,1]{0,2,3,1:T(8,128)S(1)} %copy.33), channel_id=1, source_target_pairs={{1,0},{2,1},{3,2},{0,3},{5,4},{6,5},{7,6},{4,7},{9,8},{10,9},{11,1... | collective-permute-start | bytes 16136 | tf_op jit(solution)/shard_map/ppermute | solution.py:34
  32.2 3.4 %collective-permute-start.5 = (f32[21,8,8,1]{0,2,3,1:T(8,128)S(1)}, f32[21,8,8,1]{0,2,3,1:T(8,128)S(1)}, u32[]{:S(2)}, u32[]{:S(2)}) collective-permute-start(f32[21,8,8,1]{0,2,3,1:T(8,128)S(1)} %copy.31), channel_id=1, source_target_pairs={{0,1},{1,2},{2,3},{3,0},{4,5},{5,6},{6,7},{7,4},{8,9},{9,10},{10,1... | collective-permute-start | bytes 16136 | tf_op jit(solution)/shard_map/ppermute | solution.py:33
  34.1 1.9 %copy-start.4 = (f32[20,20]{1,0:T(8,128)S(1)}, f32[20,20]{1,0:T(8,128)}, u32[]{:S(2)}) copy-start(f32[20,20]{1,0:T(8,128)} %param.17) | copy-start | bytes 4804
